TPU v7x, 1024 devices: a whole 8x8x8 slice. The times are simulated.
1024 devices in a mesh: seq: 128 (over z, y, core), head: 8 (over x).
Axes of the slice: x: 8, y: 8, z: 8, core: 2. Of those that a mesh axis runs over, the one named last changes fastest.
Arguments:
- queries: bfloat16 [65536, 4096], P(('seq', 'head')), may hold values from -6 to 6
- keys_in: bfloat16 [65536, 4096], P(('seq', 'head')), may hold values from -6 to 6
- values_in: bfloat16 [65536, 4096], P(('seq', 'head')), may hold values from -8 to 8, as said below
- gain: float32 [4096], replicated, may hold values from 0.1 to 1.9
Outputs:
- normed: bfloat16 [65536, 4096], P(('seq', 'head'))
Inputs may be any that keep to these rules, and one draw needn't show every extreme that they name: `values_in`: values of order one whose typical size differs from column to column.
All inputs are finite; a program needn't handle non-finite values.
Results may differ from a plain program's by a relative error of at most 0.0058.
Values may be sent and summed in bfloat16 or wider, within the bound.
A program may use at most 128 MiB of HBM per device.

v0:
```python
import jax
import jax.numpy as jnp
from jax import lax
from jax.sharding import PartitionSpec as P

H = 32
HD = 128
D = 4096


def entering(value, axis, join, neutral):
    count, mine = (lax.axis_size(axis), lax.axis_index(axis))
    pieces = lax.all_gather(value, axis)
    running = jnp.full_like(value, 0) + jnp.asarray(neutral, value.dtype)

    def turn(position, running):
        longer = join(running, pieces[position])
        return jnp.where(position < mine, longer, running)

    return lax.fori_loop(0, count - 1, turn, running)


def add_states(earlier, later):
    return earlier + later


def head_major(block, row_count):
    return jnp.transpose(block.reshape(row_count, H, HD), (1, 0, 2))


def local(queries, keys_in, values_in, gain):
    row_count = queries.shape[0]
    q_act = head_major(jax.nn.silu(queries.astype(jnp.float32)).astype(jnp.bfloat16), row_count)
    k_act = head_major(jax.nn.silu(keys_in.astype(jnp.float32)).astype(jnp.bfloat16), row_count)
    values = head_major(values_in, row_count)
    q_grp, k_grp, v_grp = (
        lax.all_to_all(q_act, "head", split_axis=0, concat_axis=1, tiled=True),
        lax.all_to_all(k_act, "head", split_axis=0, concat_axis=1, tiled=True),
        lax.all_to_all(values, "head", split_axis=0, concat_axis=1, tiled=True),
    )
    shard_len = q_grp.shape[1]
    positions = lax.broadcasted_iota(jnp.int32, (shard_len, shard_len), 0)
    others = lax.broadcasted_iota(jnp.int32, (shard_len, shard_len), 1)
    causal_mask = others <= positions
    scores = jnp.einsum("htd,hsd->hts", q_grp, k_grp, preferred_element_type=jnp.float32)
    weights = jnp.where(causal_mask[None], scores, 0.0).astype(jnp.bfloat16)
    intra = jnp.einsum("hts,hsd->htd", weights, v_grp, preferred_element_type=jnp.float32)
    local_state = jnp.einsum("hsd,hse->hde", k_grp, v_grp, preferred_element_type=jnp.float32)
    prefix = entering(local_state, "seq", add_states, jnp.zeros_like(local_state))
    inter = jnp.einsum(
        "htd,hde->hte", q_grp, prefix.astype(jnp.bfloat16), preferred_element_type=jnp.float32
    )
    attn = (intra + inter).astype(jnp.bfloat16)
    returned = lax.all_to_all(attn, "head", split_axis=1, concat_axis=0, tiled=True)
    widened = jnp.transpose(returned, (1, 0, 2)).reshape(row_count, D).astype(jnp.float32)
    mean_square = jnp.mean(widened * widened, axis=-1, keepdims=True)
    return (widened * lax.rsqrt(mean_square + 1e-05) * gain[None, :]).astype(jnp.bfloat16)


def solution(mesh):
    placed = (P(("seq", "head"), None), P(("seq", "head"), None), P(("seq", "head"), None), P())
    return jax.shard_map(
        local, mesh=mesh, in_specs=placed, out_specs=P(("seq", "head"), None), check_vma=False
    )
```

profile of v0, /device:TPU:1, one launch (start us, length us, event | category | flops | bytes accessed | tf_op | source)
XLA Modules:
  0.0 382.7 jit_solution(3021951166520101179)
XLA Ops:
  6.5 1.4 fusion.14
  9.0 7.4 %all-to-all-start.1 = ((bf16[32,64,128]{2,1,0:T(8,128)(2,1)}), bf16[32,64,128]{2,1,0:T(8,128)(2,1)S(1)}, u32[]{:S(2)}, u32[]{:S(2)}) async-start(bf16[32,64,128]{2,1,0:T(8,128)(2,1)} %copy.30), calls=%async_computation.1 | async-start | bytes 1048576 | tf_op jit(solution)/shard_map/all_to_all | solution.py:38
  17.6 11.0 %all-to-all-done.1 = bf16[32,64,128]{2,1,0:T(8,128)(2,1)S(1)} async-done(((bf16[32,64,128]{2,1,0:T(8,128)(2,1)}), bf16[32,64,128]{2,1,0:T(8,128)(2,1)S(1)}, u32[]{:S(2)}, u32[]{:S(2)}) %all-to-all-start.1) | async-done | bytes 524320 | tf_op jit(solution)/shard_map/all_to_all | solution.py:38
  28.6 3.5 all-to-all-start.2
  32.2 12.7 %all-to-all-done.2 = bf16[32,64,128]{2,1,0:T(8,128)(2,1)S(1)} async-done(((bf16[32,64,128]{2,1,0:T(8,128)(2,1)}), bf16[32,64,128]{2,1,0:T(8,128)(2,1)S(1)}, u32[]{:S(2)}, u32[]{:S(2)}) %all-to-all-start.2) | async-done | bytes 524320 | tf_op jit(solution)/shard_map/all_to_all | solution.py:39
  45.0 1.1 fusion.20
  47.5 3.5 all-to-all-start
  51.8 11.3 %all-to-all-done = bf16[32,64,128]{2,1,0:T(8,128)(2,1)S(1)} async-done(((bf16[32,64,128]{2,1,0:T(8,128)(2,1)}), bf16[32,64,128]{2,1,0:T(8,128)(2,1)S(1)}, u32[]{:S(2)}, u32[]{:S(2)}) %all-to-all-start) | async-done | bytes 524320 | tf_op jit(solution)/shard_map/all_to_all | solution.py:37
  63.1 149.5 %all-gather.3.cloned.1.call-done = f32[512,128,128]{2,1,0:T(8,128)} async-done(((f32[4,128,128]{2,1,0:T(8,128)}), f32[512,128,128]{2,1,0:T(8,128)}) %all-gather.3.cloned.1.call-update) | async-done | bytes 33554448 | tf_op jit(solution)/shard_map/all_gather | solution.py:13
  212.6 135.2 %while.14 = (s32[]{:T(128)}, f32[4,128,128]{2,1,0:T(8,128)S(1)}, s32[]{:T(128)}, f32[128,4,128,128]{3,2,1,0:T(8,128)}, s32[]{:T(128)}, /*index=5*/s32[]{:T(128)}) while((s32[]{:T(128)}, f32[4,128,128]{2,1,0:T(8,128)S(1)}, s32[]{:T(128)}, f32[128,4,128,128]{3,2,1,0:T(8,128)}, s32[]{:T(128)}, /*index=5*/s32[]{:T(128)}) %tuple.38), condition=%wide.region_1.2_spmd.clone, body=%wide.region_0.1_spmd.clone.sunk | while | flops 196612 | bytes 786525 | solution.py:20
  217.9 1.0 add_select_fusion.2
  219.0 1.0 add_select_fusion.2
  224.3 1.0 add_select_fusion.2
  225.4 1.0 add_select_fusion.2
  231.8 1.0 add_select_fusion.2
  232.8 1.0 add_select_fusion.2
  238.2 1.0 add_select_fusion.2
  239.2 1.0 add_select_fusion.2
  244.5 1.0 add_select_fusion.2
  245.6 1.0 add_select_fusion.2
  252.0 1.0 add_select_fusion.2
  253.1 1.0 add_select_fusion.2
  258.4 1.0 add_select_fusion.2
  259.4 1.0 add_select_fusion.2
  264.8 1.0 add_select_fusion.2
  265.8 1.0 add_select_fusion.2
  272.2 1.0 add_select_fusion.2
  273.3 1.0 add_select_fusion.2
  278.6 1.0 add_select_fusion.2
  279.7 1.0 add_select_fusion.2
  348.1 2.2 fusion.2
  350.7 23.7 %all_to_all.66 = bf16[4,512,128]{2,0,1:T(4,128)(2,1)S(1)} all-to-all(bf16[4,512,128]{2,0,1:T(4,128)(2,1)S(1)} %copy.35), channel_id=1, replica_groups=mesh['seq'=128,'head'=8] {'head'}, dimensions={1} | all-to-all | bytes 1048576 | tf_op jit(solution)/shard_map/all_to_all | solution.py:54
  (134 shorter events, 117.9 us)
Async XLA Ops:
  6.5 9.9 %copy-start = (bf16[64,4096]{1,0:T(8,128)(2,1)S(1)}, bf16[64,4096]{1,0:T(8,128)(2,1)}, u32[]{:S(2)}) copy-start(bf16[64,4096]{1,0:T(8,128)(2,1)} %param.8) | copy-start | bytes 1572868
  9.0 37.0 %copy-start.1 = (bf16[64,4096]{1,0:T(8,128)(2,1)S(1)}, bf16[64,4096]{1,0:T(8,128)(2,1)}, u32[]{:S(2)}) copy-start(bf16[64,4096]{1,0:T(8,128)(2,1)} %param.6) | copy-start | bytes 1572868
  9.0 19.6 %all-to-all-start.1 = ((bf16[32,64,128]{2,1,0:T(8,128)(2,1)}), bf16[32,64,128]{2,1,0:T(8,128)(2,1)S(1)}, u32[]{:S(2)}, u32[]{:S(2)}) async-start(bf16[32,64,128]{2,1,0:T(8,128)(2,1)} %copy.30), calls=%async_computation.1 | async-start | bytes 1048576 | tf_op jit(solution)/shard_map/all_to_all | solution.py:38
  28.6 16.3 %all-to-all-start.2 = ((bf16[32,64,128]{2,1,0:T(8,128)(2,1)}), bf16[32,64,128]{2,1,0:T(8,128)(2,1)S(1)}, u32[]{:S(2)}, u32[]{:S(2)}) async-start(bf16[32,64,128]{2,1,0:T(8,128)(2,1)} %copy.32), calls=%async_computation.2 | async-start | bytes 1048576 | tf_op jit(solution)/shard_map/all_to_all | solution.py:39
  32.1 180.5 %all-gather.3.cloned.1.call-start = ((), (), s32[]{:S(2)}) async-start(), calls=%async_computation.4 | async-start | bytes 33816576 | tf_op jit(solution)/shard_map/all_gather | solution.py:13
  47.5 15.6 %all-to-all-start = ((bf16[32,64,128]{2,1,0:T(8,128)(2,1)}), bf16[32,64,128]{2,1,0:T(8,128)(2,1)S(1)}, u32[]{:S(2)}, u32[]{:S(2)}) async-start(bf16[32,64,128]{2,1,0:T(8,128)(2,1)} %copy.28), calls=%async_computation | async-start | bytes 1048576 | tf_op jit(solution)/shard_map/all_to_all | solution.py:37
  350.3 24.6 %copy-start.2 = (f32[4096]{0:T(1024)S(1)}, f32[4096]{0:T(1024)}, u32[]{:S(2)}) copy-start(f32[4096]{0:T(1024)} %param.9) | copy-start | bytes 49156
Sparse Core Ops, SparseCore 0:
  46.2 166.3 all-gather.2
where the time goes:
time: 387 us; the launch traced here: 383 us
  waiting for transfers between devices  185 us (48%)
  other arithmetic  136 us (35%)
  blocking collectives  23.7 us (6%)
  starting transfers between devices  14.5 us (4%)
  between operations  13.6 us (4%)
  local copies, waits for them, and re-layouts  3.89 us (1%)
    all_gather x1, waiting for transfers between devices, entering(): pieces = lax.all_gather(value, axis)  150 us
    select_n x127, other arithmetic, turn(): return jnp.where(position < mine, longer, running)  132 us
    all_to_all x1, blocking collectives, local(): lax.all_to_all(attn, 'head', split_axis=1, concat_axis=0, tiled=True)  23.7 us
    all_to_all x1, waiting for transfers between devices, local(): lax.all_to_all(values, 'head', split_axis=0, concat_axis=1, tiled=True)  12.7 us
    all_to_all x1, waiting for transfers between devices, local(): lax.all_to_all(q_act, 'head', split_axis=0, concat_axis=1, tiled=True)  11.3 us
    all_to_all x1, waiting for transfers between devices, local(): lax.all_to_all(k_act, 'head', split_axis=0, concat_axis=1, tiled=True)  11 us
  transfers between devices with their start and end apart: 4, of which 4 were waited for; matrix products, arithmetic and copies ran while one was open for 1% of the time, Pallas kernels for 0%

commit v1 on v0

v1 whole, which is shorter than its diff:
```python
import functools

import jax
import jax.numpy as jnp
from jax import lax
from jax.experimental import pallas as pl
from jax.experimental.pallas import tpu as pltpu
from jax.sharding import PartitionSpec as P

HD = 128
GROUP = 16
MESH = pl.DeviceIdType.MESH
BF16, F32 = jnp.bfloat16, jnp.float32


def silu(x):
    wide = x.astype(F32)
    return (wide / (1.0 + jnp.exp(-wide))).astype(BF16)


def far_first(n):
    return sorted(range(1, n), key=lambda d: -min(d, n - d))


def kernel(nx, nz, q_hbm, k_hbm, v_hbm, gain_ref, out_ref, q_raw, k_raw, kv, q_act, kv_in, q_in, t_buf, r1, r_sum, r2,
           p_out, p_in, acc, o_buf, a_in, in_sem, kv_s, kv_r, q_s, q_r, r1_s, r1_r, r2_s, r2_r, r3_s, r3_r, o_s, o_r,
           late):
    x, s = lax.axis_index("head"), lax.axis_index("seq")
    g, z = lax.rem(s, GROUP), s // GROUP
    rows = q_raw.shape[0]
    width = kv_in.shape[-1]
    heads = width // HD
    toks = nx * rows
    piece = t_buf.shape[1] // GROUP

    def at_x(t):
        return {"head": t}

    def at_g(t):
        return {"seq": z * GROUP + t}

    def at_z(t):
        return {"seq": t * GROUP + g}

    first = (x == 0) & (s == 0)
    line_first = (s == 0) & (x != 0)
    plane_first = (x == 0) & (z == 0) & (g != 0)
    stack_first = (x == 0) & (g == 0) & (z != 0)

    loads = [
        pltpu.make_async_copy(k_hbm, k_raw, in_sem.at[0]),
        pltpu.make_async_copy(v_hbm, kv.at[1], in_sem.at[1]),
        pltpu.make_async_copy(q_hbm, q_raw, in_sem.at[2]),
    ]
    for load in loads:
        load.start()

    barrier = pltpu.get_barrier_semaphore()
    peers = ((nx, x, at_x), (GROUP, g, at_g), (nz, z, at_z))
    n_peers = sum(n - 1 for n, _, _ in peers)

    def greet(sem):
        for n, me, at in peers:
            for d in range(1, n):
                pl.semaphore_signal(sem, inc=1, device_id=at(lax.rem(me + d, n)), device_id_type=MESH)

    @pl.when(jnp.logical_not(first))
    def _():
        greet(barrier)

    loads[0].wait()
    kv[0] = silu(k_raw[...])
    loads[1].wait()

    pl.semaphore_wait(barrier, n_peers - (line_first | plane_first | stack_first).astype(jnp.int32))

    @pl.when(first)
    def _():
        greet(late)

    def columns(t, half):
        return pl.ds(pl.multiple_of(t * 2 * width + half * width, width), width)

    def kv_copy(t, half):
        return kv.at[:, :, columns(t, half)], kv_in.at[half, x], kv_s.at[half], kv_r.at[half]

    def q_copy(t, half):
        return q_act.at[:, columns(t, half)], q_in.at[half, x], q_s.at[half], q_r.at[half]

    def remote(copy, device):
        src, dst, send, recv = copy
        pltpu.make_async_remote_copy(src, dst, send, recv, device_id=device, device_id_type=MESH).start()

    def local(copy):
        src, dst, _, recv = copy
        pltpu.make_async_copy(src, dst, recv).start()

    def wait(ref, sem):
        pltpu.make_async_copy(ref, ref, sem).wait()

    def spread_x(copy_of, half, open_late):
        for d in far_first(nx):
            t = lax.rem(x + d, nx)
            if open_late:
                @pl.when(jnp.logical_not((s == 0) & (t == 0)))
                def _():
                    remote(copy_of(t, half), at_x(t))
            else:
                remote(copy_of(t, half), at_x(t))
        local(copy_of(x, half))

    spread_x(kv_copy, 0, True)
    spread_x(kv_copy, 1, True)
    loads[2].wait()
    q_act[...] = silu(q_raw[...])
    spread_x(q_copy, 0, True)
    spread_x(q_copy, 1, True)

    @pl.when(line_first | plane_first | stack_first)
    def _():
        pl.semaphore_wait(late, 1)

    @pl.when(line_first)
    def _():
        for half in range(2):
            remote(kv_copy(0, half), at_x(0))
        for half in range(2):
            remote(q_copy(0, half), at_x(0))

    def tokens(ref):
        return ref.reshape(toks, width)

    def state(half):
        wait(kv_in.at[half], kv_r.at[half])
        keys, vals = tokens(kv_in[half, :, 0]), tokens(kv_in[half, :, 1])
        for h in range(heads):
            cols = slice(h * HD, (h + 1) * HD)
            t_buf[half, cols, :] = lax.dot_general(
                keys[:, cols], vals[:, cols], (((0,), (0,)), ((), ())), preferred_element_type=F32
            )
        for d in range(GROUP):
            t = lax.rem(g + d, GROUP) if d else g
            span = pl.ds(pl.multiple_of(t * piece, piece), piece)
            copy = (t_buf.at[half, span], r1.at[half, g], r1_s.at[half], r1_r.at[half])
            if d:
                remote(copy, at_g(t))
            else:
                local(copy)

    def plane_sum(half):
        wait(r1.at[half], r1_r.at[half])
        r_sum[half] = jnp.sum(r1[half], axis=0)
        for d in range(nz):
            t = lax.rem(z + d, nz) if d else z
            copy = (r_sum.at[half], r2.at[half, z], r2_s.at[half], r2_r.at[half])
            if d:
                remote(copy, at_z(t))
            else:
                local(copy)

    def prefixes(half):
        wait(r2.at[half], r2_r.at[half])
        running = jnp.zeros(r_sum.shape[1:], F32)
        for i in range(nz):
            running = running + jnp.where(i < z, r2[half, i], 0.0)
        for j in range(GROUP):
            p_out[half, j] = running.astype(BF16)
            running = running + r1[half, j]
        for d in range(GROUP):
            t = lax.rem(g + d, GROUP) if d else g
            span = pl.ds(pl.multiple_of(g * piece, piece), piece)
            copy = (p_out.at[half, t], p_in.at[half, span], r3_s.at[half], r3_r.at[half])
            if d:
                remote(copy, at_g(t))
            else:
                local(copy)

    block = toks // 2
    causal = lax.broadcasted_iota(jnp.int32, (block, block), 1) <= lax.broadcasted_iota(jnp.int32, (block, block), 0)

    def weighted(queries, keys, vals, masked):
        scores = lax.dot_general(queries, keys, (((1,), (1,)), ((), ())), preferred_element_type=F32)
        if masked:
            scores = jnp.where(causal, scores, 0.0)
        return jnp.dot(scores.astype(BF16), vals, preferred_element_type=F32)

    def intra(half):
        wait(q_in.at[half], q_r.at[half])
        queries = tokens(q_in[half])
        keys, vals = tokens(kv_in[half, :, 0]), tokens(kv_in[half, :, 1])
        for h in range(heads):
            cols = slice(h * HD, (h + 1) * HD)
            q, k, v = queries[:, cols], keys[:, cols], vals[:, cols]
            acc[half, :block, cols] = weighted(q[:block], k[:block], v[:block], True)
            acc[half, block:, cols] = weighted(q[block:], k[block:], v[block:], True) + weighted(
                q[block:], k[:block], v[:block], False
            )

    def finish(half):
        wait(p_in.at[half], r3_r.at[half])
        queries = tokens(q_in[half])
        for h in range(heads):
            cols = slice(h * HD, (h + 1) * HD)
            inter = jnp.dot(queries[:, cols], p_in[half, cols, :], preferred_element_type=F32)
            o_buf[half, :, :, cols] = (acc[half, :, cols] + inter).astype(BF16).reshape(nx, rows, HD)

        def o_copy(t, half):
            return o_buf.at[half, t], a_in.at[:, columns(x, half)], o_s.at[half], o_r.at[half]

        spread_x(o_copy, half, False)

    state(0)
    plane_sum(0)
    state(1)
    prefixes(0)
    plane_sum(1)
    intra(0)
    finish(0)
    prefixes(1)
    intra(1)
    finish(1)

    for half in range(2):
        wait(a_in.at[:, pl.ds(0, nx * width)], o_r.at[half])
    wide = a_in[...].astype(F32)
    mean_square = jnp.mean(wide * wide, axis=-1, keepdims=True)
    out_ref[...] = (wide * lax.rsqrt(mean_square + 1e-05) * gain_ref[...]).astype(BF16)

    for half in range(2):
        wait(kv_in.at[half, pl.ds(0, nx - 1)], kv_s.at[half])
        wait(q_in.at[half, pl.ds(0, nx - 1)], q_s.at[half])
        wait(o_buf.at[half, pl.ds(0, nx - 1)], o_s.at[half])
        wait(r1.at[half, pl.ds(0, GROUP - 1)], r1_s.at[half])
        wait(r2.at[half, pl.ds(0, nz - 1)], r2_s.at[half])
        wait(p_out.at[half, pl.ds(0, GROUP - 1)], r3_s.at[half])


def solution(mesh):
    nx, nz = mesh.shape["head"], mesh.shape["seq"] // GROUP

    def local(queries, keys_in, values_in, gain):
        rows, d = queries.shape
        width = d // nx // 2
        piece = width // GROUP
        vmem, pair = pltpu.VMEM, pltpu.SemaphoreType.DMA((2,))
        return pl.pallas_call(
            functools.partial(kernel, nx, nz),
            out_shape=jax.ShapeDtypeStruct((rows, d), BF16),
            in_specs=[pl.BlockSpec(memory_space=pl.ANY)] * 3 + [pl.BlockSpec(memory_space=pltpu.VMEM)],
            out_specs=pl.BlockSpec(memory_space=pltpu.VMEM),
            scratch_shapes=[
                vmem((rows, d), BF16),
                vmem((rows, d), BF16),
                vmem((2, rows, d), BF16),
                vmem((rows, d), BF16),
                vmem((2, nx, 2, rows, width), BF16),
                vmem((2, nx, rows, width), BF16),
                vmem((2, width, HD), F32),
                vmem((2, GROUP, piece, HD), F32),
                vmem((2, piece, HD), F32),
                vmem((2, nz, piece, HD), F32),
                vmem((2, GROUP, piece, HD), BF16),
                vmem((2, width, HD), BF16),
                vmem((2, nx * rows, width), F32),
                vmem((2, nx, rows, width), BF16),
                vmem((rows, d), BF16),
                pltpu.SemaphoreType.DMA((3,)),
            ]
            + [pair] * 12
            + [pltpu.SemaphoreType.REGULAR],
            compiler_params=pltpu.CompilerParams(
                collective_id=0, has_side_effects=True, vmem_limit_bytes=40 * 2**20
            ),
        )(queries, keys_in, values_in, gain.reshape(1, d))

    placed = P(("seq", "head"), None)
    return jax.shard_map(
        local, mesh=mesh, in_specs=(placed, placed, placed, P()), out_specs=placed, check_vma=False
    )
```

time: 387 us -> 83.3 us (0.22)
  waiting for transfers between devices: 185 us -> 0 us
  other arithmetic: 136 us -> 0 us
  Pallas kernels: 0 us -> 77.6 us
  blocking collectives: 23.7 us -> 0 us
  starting transfers between devices: 14.5 us -> 0 us
  between operations: 13.6 us -> 0.01 us
    all_gather x1 -> x0, waiting for transfers between devices: 150 us -> none  [entering(): pieces = lax.all_gather(value, axis)]
    select_n x127 -> x0, other arithmetic: 132 us -> none  [turn(): return jnp.where(position < mine, longer, running)]
    pallas_call x0 -> x1, Pallas kernels: none -> 77.6 us  [local(): pl.pallas_call(functools.partial(kernel, nx, nz), out_shape=jax.ShapeDtyp...]
    all_to_all x3 -> x0, waiting for transfers between devices: 35.1 us -> none  [the longest x1 12.7 us: local(): lax.all_to_all(values, 'head', split_axis=0, concat_axis=1, tiled=True)]
    all_to_all x1 -> x0, blocking collectives: 23.7 us -> none  [local(): lax.all_to_all(attn, 'head', split_axis=1, concat_axis=0, tiled=True)]
    all_to_all x3 -> x0, starting transfers between devices: 14.4 us -> none  [the longest x1 7.44 us: local(): lax.all_to_all(k_act, 'head', split_axis=0, concat_axis=1, tiled=True)]
    unnamed x9, local copies, waits for them, and re-layouts: 0.28 us -> 4.64 us
  transfers between devices with their start and end apart: 4 -> 0, of which waited for: 4 -> 0; matrix products, arithmetic and copies ran while one was open for 1% -> 0% of each run, Pallas kernels for 0% -> 0%
where the time goes in v1:
time: 83.3 us; the launch traced here: 82.3 us
  Pallas kernels  77.6 us (93%)
  local copies, waits for them, and re-layouts  4.64 us (6%)
    pallas_call x1, Pallas kernels, local(): pl.pallas_call(functools.partial(kernel, nx, nz), out_shape=jax.ShapeDtyp...  77.6 us
    unnamed x9, local copies, waits for them, and re-layouts  4.64 us

profile of v1, /device:TPU:1, one launch (start us, length us, event | category | flops | bytes accessed | tf_op | source)
XLA Modules:
  0.0 82.3 jit_solution(6452821954706498443)
XLA Ops:
  0.0 0.0 copy-start
  0.0 1.0 %copy-done = bf16[64,4096]{1,0:T(8,128)(2,1)S(1)} copy-done((bf16[64,4096]{1,0:T(8,128)(2,1)S(1)}, bf16[64,4096]{1,0:T(8,128)(2,1)}, u32[]{:S(2)}) %copy-start) | copy-done | bytes 524312
  1.0 0.0 copy-start.1
  1.0 1.0 %copy-done.1 = bf16[64,4096]{1,0:T(8,128)(2,1)S(1)} copy-done((bf16[64,4096]{1,0:T(8,128)(2,1)S(1)}, bf16[64,4096]{1,0:T(8,128)(2,1)}, u32[]{:S(2)}) %copy-start.1) | copy-done | bytes 524312
  2.1 0.0 copy-start.2
  2.1 1.0 %copy-done.2 = bf16[64,4096]{1,0:T(8,128)(2,1)S(1)} copy-done((bf16[64,4096]{1,0:T(8,128)(2,1)S(1)}, bf16[64,4096]{1,0:T(8,128)(2,1)}, u32[]{:S(2)}) %copy-start.2) | copy-done | bytes 524312
  3.1 0.0 copy-start.3
  3.1 0.7 copy-done.3
  3.8 77.6 %shard_map.46 = bf16[64,4096]{1,0:T(8,128)(2,1)S(1)} custom-call(bf16[64,4096]{1,0:T(8,128)(2,1)S(1)} %copy-done, bf16[64,4096]{1,0:T(8,128)(2,1)S(1)} %copy-done.1, bf16[64,4096]{1,0:T(8,128)(2,1)S(1)} %copy-done.2, f32[1,4096]{1,0:T(1,128)S(1)} %bitcast.1), custom_call_target="tpu_custom_call" | custom-call | tf_op jit(solution)/shard_map/pallas_call | solution.py:246
  81.5 0.8 copy.6
Async XLA Ops:
  0.0 1.0 %copy-start = (bf16[64,4096]{1,0:T(8,128)(2,1)S(1)}, bf16[64,4096]{1,0:T(8,128)(2,1)}, u32[]{:S(2)}) copy-start(bf16[64,4096]{1,0:T(8,128)(2,1)} %q_hbm.1) | copy-start | bytes 1572868
  1.0 1.0 %copy-start.1 = (bf16[64,4096]{1,0:T(8,128)(2,1)S(1)}, bf16[64,4096]{1,0:T(8,128)(2,1)}, u32[]{:S(2)}) copy-start(bf16[64,4096]{1,0:T(8,128)(2,1)} %k_hbm.1) | copy-start | bytes 1572868
  2.1 1.0 %copy-start.2 = (bf16[64,4096]{1,0:T(8,128)(2,1)S(1)}, bf16[64,4096]{1,0:T(8,128)(2,1)}, u32[]{:S(2)}) copy-start(bf16[64,4096]{1,0:T(8,128)(2,1)} %v_hbm.1) | copy-start | bytes 1572868
  3.1 0.7 copy-start.3

commit v2 on v1

--- a/solution.py
+++ b/solution.py
@@ -22,9 +22,9 @@
     return sorted(range(1, n), key=lambda d: -min(d, n - d))
 
 
-def kernel(nx, nz, q_hbm, k_hbm, v_hbm, gain_ref, out_ref, q_raw, k_raw, kv, q_act, kv_in, q_in, t_buf, r1, r_sum, r2,
-           p_out, p_in, acc, o_buf, a_in, in_sem, kv_s, kv_r, q_s, q_r, r1_s, r1_r, r2_s, r2_r, r3_s, r3_r, o_s, o_r,
-           late):
+def kernel(nx, nz, q_hbm, k_hbm, v_hbm, attn, scale, q_raw, k_raw, kv, q_act, kv_in, q_in, t_buf, r1, r_sum, r2,
+           below, p_out, p_in, acc, o_buf, in_sem, kv_s, kv_r, q_s, q_r, r1_s, r1_r, r2_s, r2_r, r3_s, r3_r, o_s, o_r,
+           late, above):
     x, s = lax.axis_index("head"), lax.axis_index("seq")
     g, z = lax.rem(s, GROUP), s // GROUP
     rows = q_raw.shape[0]
@@ -45,7 +45,6 @@
     first = (x == 0) & (s == 0)
     line_first = (s == 0) & (x != 0)
     plane_first = (x == 0) & (z == 0) & (g != 0)
-    stack_first = (x == 0) & (g == 0) & (z != 0)
 
     loads = [
         pltpu.make_async_copy(k_hbm, k_raw, in_sem.at[0]),
@@ -56,8 +55,7 @@
         load.start()
 
     barrier = pltpu.get_barrier_semaphore()
-    peers = ((nx, x, at_x), (GROUP, g, at_g), (nz, z, at_z))
-    n_peers = sum(n - 1 for n, _, _ in peers)
+    peers = ((nx, x, at_x), (GROUP, g, at_g))
 
     def greet(sem):
         for n, me, at in peers:
@@ -68,15 +66,25 @@
     def _():
         greet(barrier)
 
+    for i in range(1, nz):
+        @pl.when(i > z)
+        def _():
+            pl.semaphore_signal(barrier, inc=1, device_id=at_z(i), device_id_type=MESH)
+
     loads[0].wait()
     kv[0] = silu(k_raw[...])
     loads[1].wait()
 
-    pl.semaphore_wait(barrier, n_peers - (line_first | plane_first | stack_first).astype(jnp.int32))
+    pl.semaphore_wait(barrier, nx + GROUP - 2 + z - (line_first | plane_first).astype(jnp.int32))
 
     @pl.when(first)
     def _():
         greet(late)
+
+    for i in range(nz - 1):
+        @pl.when(i < z)
+        def _():
+            pl.semaphore_signal(above, inc=1, device_id=at_z(i), device_id_type=MESH)
 
     def columns(t, half):
         return pl.ds(pl.multiple_of(t * 2 * width + half * width, width), width)
@@ -110,22 +118,20 @@
         local(copy_of(x, half))
 
     spread_x(kv_copy, 0, True)
-    spread_x(kv_copy, 1, True)
     loads[2].wait()
     q_act[...] = silu(q_raw[...])
-    spread_x(q_copy, 0, True)
-    spread_x(q_copy, 1, True)
-
-    @pl.when(line_first | plane_first | stack_first)
+
+    @pl.when(line_first | plane_first)
     def _():
         pl.semaphore_wait(late, 1)
 
     @pl.when(line_first)
     def _():
-        for half in range(2):
-            remote(kv_copy(0, half), at_x(0))
-        for half in range(2):
-            remote(q_copy(0, half), at_x(0))
+        remote(kv_copy(0, 0), at_x(0))
+
+    spread_x(kv_copy, 1, False)
+    spread_x(q_copy, 0, False)
+    spread_x(q_copy, 1, False)
 
     def tokens(ref):
         return ref.reshape(toks, width)
@@ -150,19 +156,24 @@
     def plane_sum(half):
         wait(r1.at[half], r1_r.at[half])
         r_sum[half] = jnp.sum(r1[half], axis=0)
-        for d in range(nz):
-            t = lax.rem(z + d, nz) if d else z
-            copy = (r_sum.at[half], r2.at[half, z], r2_s.at[half], r2_r.at[half])
-            if d:
-                remote(copy, at_z(t))
-            else:
-                local(copy)
+        if half == 0:
+            @pl.when(z < nz - 1)
+            def _():
+                pl.semaphore_wait(above, nz - 1 - z)
+
+        for i in range(1, nz):
+            @pl.when(i > z)
+            def _():
+                remote((r_sum.at[half], r2.at[half, z], r2_s.at[half, i], r2_r.at[half, z]), at_z(i))
 
     def prefixes(half):
-        wait(r2.at[half], r2_r.at[half])
-        running = jnp.zeros(r_sum.shape[1:], F32)
-        for i in range(nz):
-            running = running + jnp.where(i < z, r2[half, i], 0.0)
+        below[half] = jnp.zeros(r_sum.shape[1:], F32)
+        for i in range(nz - 1):
+            @pl.when(i < z)
+            def _():
+                wait(r2.at[half, i], r2_r.at[half, i])
+                below[half] += r2[half, i]
+        running = below[half]
         for j in range(GROUP):
             p_out[half, j] = running.astype(BF16)
             running = running + r1[half, j]
@@ -205,7 +216,7 @@
             o_buf[half, :, :, cols] = (acc[half, :, cols] + inter).astype(BF16).reshape(nx, rows, HD)
 
         def o_copy(t, half):
-            return o_buf.at[half, t], a_in.at[:, columns(x, half)], o_s.at[half], o_r.at[half]
+            return o_buf.at[half, t], attn.at[:, columns(x, half)], o_s.at[half], o_r.at[half]
 
         spread_x(o_copy, half, False)
 
@@ -221,18 +232,20 @@
     finish(1)
 
     for half in range(2):
-        wait(a_in.at[:, pl.ds(0, nx * width)], o_r.at[half])
-    wide = a_in[...].astype(F32)
-    mean_square = jnp.mean(wide * wide, axis=-1, keepdims=True)
-    out_ref[...] = (wide * lax.rsqrt(mean_square + 1e-05) * gain_ref[...]).astype(BF16)
+        wait(attn.at[:, pl.ds(0, nx * width)], o_r.at[half])
+    wide = attn[...].astype(F32)
+    scale[...] = lax.rsqrt(jnp.mean(wide * wide, axis=-1, keepdims=True) + 1e-05)
 
     for half in range(2):
         wait(kv_in.at[half, pl.ds(0, nx - 1)], kv_s.at[half])
         wait(q_in.at[half, pl.ds(0, nx - 1)], q_s.at[half])
         wait(o_buf.at[half, pl.ds(0, nx - 1)], o_s.at[half])
         wait(r1.at[half, pl.ds(0, GROUP - 1)], r1_s.at[half])
-        wait(r2.at[half, pl.ds(0, nz - 1)], r2_s.at[half])
         wait(p_out.at[half, pl.ds(0, GROUP - 1)], r3_s.at[half])
+        for i in range(1, nz):
+            @pl.when(i > z)
+            def _():
+                wait(r_sum.at[half], r2_s.at[half, i])
 
 
 def solution(mesh):
@@ -243,11 +256,11 @@
         width = d // nx // 2
         piece = width // GROUP
         vmem, pair = pltpu.VMEM, pltpu.SemaphoreType.DMA((2,))
-        return pl.pallas_call(
+        attn, scale = pl.pallas_call(
             functools.partial(kernel, nx, nz),
-            out_shape=jax.ShapeDtypeStruct((rows, d), BF16),
-            in_specs=[pl.BlockSpec(memory_space=pl.ANY)] * 3 + [pl.BlockSpec(memory_space=pltpu.VMEM)],
-            out_specs=pl.BlockSpec(memory_space=pltpu.VMEM),
+            out_shape=(jax.ShapeDtypeStruct((rows, d), BF16), jax.ShapeDtypeStruct((rows, 1), F32)),
+            in_specs=[pl.BlockSpec(memory_space=pltpu.HBM)] * 3,
+            out_specs=(pl.BlockSpec(memory_space=pltpu.VMEM),) * 2,
             scratch_shapes=[
                 vmem((rows, d), BF16),
                 vmem((rows, d), BF16),
@@ -259,19 +272,22 @@
                 vmem((2, GROUP, piece, HD), F32),
                 vmem((2, piece, HD), F32),
                 vmem((2, nz, piece, HD), F32),
+                vmem((2, piece, HD), F32),
                 vmem((2, GROUP, piece, HD), BF16),
                 vmem((2, width, HD), BF16),
                 vmem((2, nx * rows, width), F32),
                 vmem((2, nx, rows, width), BF16),
-                vmem((rows, d), BF16),
                 pltpu.SemaphoreType.DMA((3,)),
             ]
-            + [pair] * 12
-            + [pltpu.SemaphoreType.REGULAR],
+            + [pair] * 6
+            + [pltpu.SemaphoreType.DMA((2, nz))] * 2
+            + [pair] * 4
+            + [pltpu.SemaphoreType.REGULAR] * 2,
             compiler_params=pltpu.CompilerParams(
-                collective_id=0, has_side_effects=True, vmem_limit_bytes=40 * 2**20
+                collective_id=0, has_side_effects=True, vmem_limit_bytes=55836672
             ),
-        )(queries, keys_in, values_in, gain.reshape(1, d))
+        )(queries, keys_in, values_in)
+        return (attn.astype(F32) * scale * gain[None, :]).astype(BF16)
 
     placed = P(("seq", "head"), None)
     return jax.shard_map(

time: 83.3 us -> 62.9 us (0.76)
  Pallas kernels: 77.6 us -> 60.9 us
  local copies, waits for them, and re-layouts: 4.64 us -> 0.6 us
  other arithmetic: 0 us -> 1.09 us
    pallas_call x1, Pallas kernels: 77.6 us -> 60.9 us  [local(): pl.pallas_call(functools.partial(kernel, nx, nz), out_shape=(jax.ShapeDty...]
    unnamed x9 -> x2, local copies, waits for them, and re-layouts: 4.64 us -> 0.6 us
    convert_element_type x0 -> x1, other arithmetic: none -> 0.98 us  [local(): return (attn.astype(F32) * scale * gain[None, :]).astype(BF16)]
where the time goes in v2:
time: 62.9 us; the launch traced here: 62.7 us
  Pallas kernels  60.9 us (97%)
  other arithmetic  1.09 us (2%)
    pallas_call x1, Pallas kernels, local(): pl.pallas_call(functools.partial(kernel, nx, nz), out_shape=(jax.ShapeDty...  60.9 us

profile of v2, /device:TPU:1, one launch (start us, length us, event | category | flops | bytes accessed | tf_op | source)
XLA Modules:
  0.0 62.7 jit_solution(13048044619487728698)
XLA Ops:
  0.0 60.9 %shard_map.46 = (bf16[64,4096]{1,0:T(8,128)(2,1)S(1)}, f32[64,1]{1,0:T(8,128)S(1)}) custom-call(bf16[64,4096]{1,0:T(8,128)(2,1)} %q_hbm.1, bf16[64,4096]{1,0:T(8,128)(2,1)} %k_hbm.1, bf16[64,4096]{1,0:T(8,128)(2,1)} %v_hbm.1), custom_call_target="tpu_custom_call" | custom-call | tf_op jit(solution)/shard_map/pallas_call | solution.py:259
  61.0 0.0 copy-start
  61.0 0.1 reduce
  61.1 0.6 copy-done
  61.7 1.0 %multiply_convert_fusion = bf16[64,4096]{1,0:T(8,128)(2,1)} fusion(bf16[64,4096]{1,0:T(8,128)(2,1)S(1)} %get-tuple-element.7, f32[4096]{0:T(1024)S(1)} %copy-done, f32[64]{0:T(128)S(1)} %reduce), kind=kLoop, calls=%fused_computation | loop fusion | flops 1048576 | bytes 1065216 | tf_op jit(solution)/shard_map/convert_element_type | solution.py:290
Async XLA Ops:
  61.0 0.7 %copy-start = (f32[4096]{0:T(1024)S(1)}, f32[4096]{0:T(1024)}, u32[]{:S(2)}) copy-start(f32[4096]{0:T(1024)} %param.7) | copy-start | bytes 49156

commit v3 on v2

--- a/solution.py
+++ b/solution.py
@@ -22,13 +22,13 @@
     return sorted(range(1, n), key=lambda d: -min(d, n - d))
 
 
-def kernel(nx, nz, q_hbm, k_hbm, v_hbm, attn, scale, q_raw, k_raw, kv, q_act, kv_in, q_in, t_buf, r1, r_sum, r2,
-           below, p_out, p_in, acc, o_buf, in_sem, kv_s, kv_r, q_s, q_r, r1_s, r1_r, r2_s, r2_r, r3_s, r3_r, o_s, o_r,
+def kernel(nx, nz, q_hbm, k_hbm, v_hbm, attn, scale, q_raw, k_raw, k_act, q_act, v_in, k_in, q_in, t_buf, r1, r_sum, r2,
+           below, p_out, p_in, acc, o_buf, in_sem, v_s, v_r, k_s, k_r, q_s, q_r, r1_s, r1_r, r2_s, r2_r, r3_s, r3_r, o_s, o_r,
            late, above):
     x, s = lax.axis_index("head"), lax.axis_index("seq")
     g, z = lax.rem(s, GROUP), s // GROUP
     rows = q_raw.shape[0]
-    width = kv_in.shape[-1]
+    width = k_in.shape[-1]
     heads = width // HD
     toks = nx * rows
     piece = t_buf.shape[1] // GROUP
@@ -48,8 +48,7 @@
 
     loads = [
         pltpu.make_async_copy(k_hbm, k_raw, in_sem.at[0]),
-        pltpu.make_async_copy(v_hbm, kv.at[1], in_sem.at[1]),
-        pltpu.make_async_copy(q_hbm, q_raw, in_sem.at[2]),
+        pltpu.make_async_copy(q_hbm, q_raw, in_sem.at[1]),
     ]
     for load in loads:
         load.start()
@@ -71,10 +70,6 @@
         def _():
             pl.semaphore_signal(barrier, inc=1, device_id=at_z(i), device_id_type=MESH)
 
-    loads[0].wait()
-    kv[0] = silu(k_raw[...])
-    loads[1].wait()
-
     pl.semaphore_wait(barrier, nx + GROUP - 2 + z - (line_first | plane_first).astype(jnp.int32))
 
     @pl.when(first)
@@ -89,11 +84,19 @@
     def columns(t, half):
         return pl.ds(pl.multiple_of(t * 2 * width + half * width, width), width)
 
-    def kv_copy(t, half):
-        return kv.at[:, :, columns(t, half)], kv_in.at[half, x], kv_s.at[half], kv_r.at[half]
+    def v_copy(t, half):
+        return v_hbm.at[:, columns(t, half)], v_in.at[half, x], v_s.at[half], v_r.at[half]
+
+    def k_copy(t, half):
+        return k_act.at[:, columns(t, half)], k_in.at[half, x], k_s.at[half], k_r.at[half]
 
     def q_copy(t, half):
         return q_act.at[:, columns(t, half)], q_in.at[half, x], q_s.at[half], q_r.at[half]
+
+    def activate(raw, act, half):
+        for t in range(nx):
+            cols = slice((2 * t + half) * width, (2 * t + half + 1) * width)
+            act[:, cols] = silu(raw[:, cols])
 
     def remote(copy, device):
         src, dst, send, recv = copy
@@ -117,9 +120,11 @@
                 remote(copy_of(t, half), at_x(t))
         local(copy_of(x, half))
 
-    spread_x(kv_copy, 0, True)
-    loads[2].wait()
-    q_act[...] = silu(q_raw[...])
+    spread_x(v_copy, 0, True)
+    loads[0].wait()
+    activate(k_raw, k_act, 0)
+    spread_x(k_copy, 0, True)
+    activate(k_raw, k_act, 1)
 
     @pl.when(line_first | plane_first)
     def _():
@@ -127,18 +132,23 @@
 
     @pl.when(line_first)
     def _():
-        remote(kv_copy(0, 0), at_x(0))
-
-    spread_x(kv_copy, 1, False)
-    spread_x(q_copy, 0, False)
-    spread_x(q_copy, 1, False)
+        remote(v_copy(0, 0), at_x(0))
+        remote(k_copy(0, 0), at_x(0))
+
+    spread_x(v_copy, 1, False)
+    spread_x(k_copy, 1, False)
+    loads[1].wait()
+    for half in range(2):
+        activate(q_raw, q_act, half)
+        spread_x(q_copy, half, False)
 
     def tokens(ref):
         return ref.reshape(toks, width)
 
     def state(half):
-        wait(kv_in.at[half], kv_r.at[half])
-        keys, vals = tokens(kv_in[half, :, 0]), tokens(kv_in[half, :, 1])
+        wait(v_in.at[half], v_r.at[half])
+        wait(k_in.at[half], k_r.at[half])
+        keys, vals = tokens(k_in[half]), tokens(v_in[half])
         for h in range(heads):
             cols = slice(h * HD, (h + 1) * HD)
             t_buf[half, cols, :] = lax.dot_general(
@@ -198,7 +208,7 @@
     def intra(half):
         wait(q_in.at[half], q_r.at[half])
         queries = tokens(q_in[half])
-        keys, vals = tokens(kv_in[half, :, 0]), tokens(kv_in[half, :, 1])
+        keys, vals = tokens(k_in[half]), tokens(v_in[half])
         for h in range(heads):
             cols = slice(h * HD, (h + 1) * HD)
             q, k, v = queries[:, cols], keys[:, cols], vals[:, cols]
@@ -220,24 +230,26 @@
 
         spread_x(o_copy, half, False)
 
-    state(0)
-    plane_sum(0)
-    state(1)
-    prefixes(0)
-    plane_sum(1)
-    intra(0)
-    finish(0)
-    prefixes(1)
-    intra(1)
-    finish(1)
-
+    for half in range(2):
+        state(half)
+        plane_sum(half)
+        prefixes(half)
+    for half in range(2):
+        intra(half)
+        finish(half)
+
+    squares = jnp.zeros((rows, width), F32)
     for half in range(2):
         wait(attn.at[:, pl.ds(0, nx * width)], o_r.at[half])
-    wide = attn[...].astype(F32)
-    scale[...] = lax.rsqrt(jnp.mean(wide * wide, axis=-1, keepdims=True) + 1e-05)
-
-    for half in range(2):
-        wait(kv_in.at[half, pl.ds(0, nx - 1)], kv_s.at[half])
+        for t in range(nx):
+            wide = attn[:, (2 * t + half) * width : (2 * t + half + 1) * width].astype(F32)
+            squares = squares + wide * wide
+    mean_square = jnp.sum(squares, axis=-1, keepdims=True) / attn.shape[1]
+    scale[...] = lax.rsqrt(mean_square + 1e-05)
+
+    for half in range(2):
+        wait(v_in.at[half, pl.ds(0, nx - 1)], v_s.at[half])
+        wait(k_in.at[half, pl.ds(0, nx - 1)], k_s.at[half])
         wait(q_in.at[half, pl.ds(0, nx - 1)], q_s.at[half])
         wait(o_buf.at[half, pl.ds(0, nx - 1)], o_s.at[half])
         wait(r1.at[half, pl.ds(0, GROUP - 1)], r1_s.at[half])
@@ -264,9 +276,10 @@
             scratch_shapes=[
                 vmem((rows, d), BF16),
                 vmem((rows, d), BF16),
-                vmem((2, rows, d), BF16),
                 vmem((rows, d), BF16),
-                vmem((2, nx, 2, rows, width), BF16),
+                vmem((rows, d), BF16),
+                vmem((2, nx, rows, width), BF16),
+                vmem((2, nx, rows, width), BF16),
                 vmem((2, nx, rows, width), BF16),
                 vmem((2, width, HD), F32),
                 vmem((2, GROUP, piece, HD), F32),
@@ -277,9 +290,9 @@
                 vmem((2, width, HD), BF16),
                 vmem((2, nx * rows, width), F32),
                 vmem((2, nx, rows, width), BF16),
-                pltpu.SemaphoreType.DMA((3,)),
+                pltpu.SemaphoreType.DMA((2,)),
             ]
-            + [pair] * 6
+            + [pair] * 8
             + [pltpu.SemaphoreType.DMA((2, nz))] * 2
             + [pair] * 4
             + [pltpu.SemaphoreType.REGULAR] * 2,

time: 62.9 us -> 61 us (0.970)
  Pallas kernels: 60.9 us -> 58.7 us
    pallas_call x1, Pallas kernels: 60.9 us -> 58.7 us  [local(): pl.pallas_call(functools.partial(kernel, nx, nz), out_shape=(jax.ShapeDty...]
where the time goes in v3:
time: 61 us; the launch traced here: 60.5 us
  Pallas kernels  58.7 us (96%)
  other arithmetic  1.09 us (2%)
    pallas_call x1, Pallas kernels, local(): pl.pallas_call(functools.partial(kernel, nx, nz), out_shape=(jax.ShapeDty...  58.7 us

profile of v3, /device:TPU:1, one launch (start us, length us, event | category | flops | bytes accessed | tf_op | source)
XLA Modules:
  0.0 60.5 jit_solution(9874019826852415271)
XLA Ops:
  0.0 58.7 %shard_map.46 = (bf16[64,4096]{1,0:T(8,128)(2,1)S(1)}, f32[64,1]{1,0:T(8,128)S(1)}) custom-call(bf16[64,4096]{1,0:T(8,128)(2,1)} %q_hbm.1, bf16[64,4096]{1,0:T(8,128)(2,1)} %k_hbm.1, bf16[64,4096]{1,0:T(8,128)(2,1)} %v_hbm.1), custom_call_target="tpu_custom_call" | custom-call | tf_op jit(solution)/shard_map/pallas_call | solution.py:271
  58.8 0.0 copy-start
  58.8 0.1 reduce
  58.9 0.6 copy-done
  59.5 1.0 %multiply_convert_fusion = bf16[64,4096]{1,0:T(8,128)(2,1)} fusion(bf16[64,4096]{1,0:T(8,128)(2,1)S(1)} %get-tuple-element.7, f32[4096]{0:T(1024)S(1)} %copy-done, f32[64]{0:T(128)S(1)} %reduce), kind=kLoop, calls=%fused_computation | loop fusion | flops 1048576 | bytes 1065216 | tf_op jit(solution)/shard_map/convert_element_type | solution.py:303
Async XLA Ops:
  58.8 0.7 %copy-start = (f32[4096]{0:T(1024)S(1)}, f32[4096]{0:T(1024)}, u32[]{:S(2)}) copy-start(f32[4096]{0:T(1024)} %param.7) | copy-start | bytes 49156

commit v4 on v3

--- a/solution.py
+++ b/solution.py
@@ -45,6 +45,7 @@
     first = (x == 0) & (s == 0)
     line_first = (s == 0) & (x != 0)
     plane_first = (x == 0) & (z == 0) & (g != 0)
+    stack_first = (x == 0) & (g == 0) & (z != 0)
 
     loads = [
         pltpu.make_async_copy(k_hbm, k_raw, in_sem.at[0]),
@@ -65,19 +66,20 @@
     def _():
         greet(barrier)
 
-    for i in range(1, nz):
-        @pl.when(i > z)
+    for i in range(nz):
+        @pl.when((i > z) & jnp.logical_not(first) | (i == 0) & stack_first)
         def _():
             pl.semaphore_signal(barrier, inc=1, device_id=at_z(i), device_id_type=MESH)
 
-    pl.semaphore_wait(barrier, nx + GROUP - 2 + z - (line_first | plane_first).astype(jnp.int32))
+    stack_below = jnp.where(first, nz - 1, z - stack_first.astype(jnp.int32))
+    pl.semaphore_wait(barrier, nx + GROUP - 2 + stack_below - (line_first | plane_first).astype(jnp.int32))
 
     @pl.when(first)
     def _():
         greet(late)
 
     for i in range(nz - 1):
-        @pl.when(i < z)
+        @pl.when((i < z) & jnp.logical_not(stack_first & (i == 0)))
         def _():
             pl.semaphore_signal(above, inc=1, device_id=at_z(i), device_id_type=MESH)
 
@@ -167,7 +169,7 @@
         wait(r1.at[half], r1_r.at[half])
         r_sum[half] = jnp.sum(r1[half], axis=0)
         if half == 0:
-            @pl.when(z < nz - 1)
+            @pl.when((z < nz - 1) & jnp.logical_not(first))
             def _():
                 pl.semaphore_wait(above, nz - 1 - z)
 

time: 61 us -> 61.3 us (level)
  Pallas kernels: 58.7 us -> 59.4 us
    pallas_call x1, Pallas kernels: 58.7 us -> 59.4 us  [local(): pl.pallas_call(functools.partial(kernel, nx, nz), out_shape=(jax.ShapeDty...]
where the time goes in v4:
time: 61.3 us; the launch traced here: 61.1 us
  Pallas kernels  59.4 us (97%)
  other arithmetic  1.09 us (2%)
    pallas_call x1, Pallas kernels, local(): pl.pallas_call(functools.partial(kernel, nx, nz), out_shape=(jax.ShapeDty...  59.4 us

profile of v4, /device:TPU:1, one launch (start us, length us, event | category | flops | bytes accessed | tf_op | source)
XLA Modules:
  0.0 61.1 jit_solution(969554628769837059)
XLA Ops:
  0.0 59.4 %shard_map.46 = (bf16[64,4096]{1,0:T(8,128)(2,1)S(1)}, f32[64,1]{1,0:T(8,128)S(1)}) custom-call(bf16[64,4096]{1,0:T(8,128)(2,1)} %q_hbm.1, bf16[64,4096]{1,0:T(8,128)(2,1)} %k_hbm.1, bf16[64,4096]{1,0:T(8,128)(2,1)} %v_hbm.1), custom_call_target="tpu_custom_call" | custom-call | tf_op jit(solution)/shard_map/pallas_call | solution.py:273
  59.4 0.0 copy-start
  59.4 0.1 reduce
  59.6 0.6 copy-done
  60.2 1.0 %multiply_convert_fusion = bf16[64,4096]{1,0:T(8,128)(2,1)} fusion(bf16[64,4096]{1,0:T(8,128)(2,1)S(1)} %get-tuple-element.7, f32[4096]{0:T(1024)S(1)} %copy-done, f32[64]{0:T(128)S(1)} %reduce), kind=kLoop, calls=%fused_computation | loop fusion | flops 1048576 | bytes 1065216 | tf_op jit(solution)/shard_map/convert_element_type | solution.py:305
Async XLA Ops:
  59.4 0.7 %copy-start = (f32[4096]{0:T(1024)S(1)}, f32[4096]{0:T(1024)}, u32[]{:S(2)}) copy-start(f32[4096]{0:T(1024)} %param.7) | copy-start | bytes 49156
